TPU v7x, 32 devices: a whole 2x2x4 slice. The times are simulated.
32 devices in a mesh: gx: 4 (over z), gy: 4 (over y, x), ta: 2 (over core).
Axes of the slice: x: 2, y: 2, z: 4, core: 2. Of those that a mesh axis runs over, the one named last changes fastest.
Arguments:
- prior_heads: float32 [64, 8, 32, 128], P('ta', 'gx', 'gy')
- facies: int32 [8, 32, 128], P('gx', 'gy'), may hold values from 0 to 5
- facies_cond: float32 [6], replicated, may hold values from 0.1 to 2
- well_cell: int32 [64], P('ta'), may hold values from 0 to 32767, as said below
- pump_rate: float32 [64], P('ta'), may hold values from 1 to 10
- obs_test: int32 [192], P('ta'), may hold values from 0 to 63, as said below
- obs_pair: int32 [192], P('ta'), may hold values from 0 to 63, as said below
Outputs:
- heads: float32 [64, 8, 32, 128], P('ta', 'gx', 'gy')
- jjt: float32 [192, 192], P('ta', ('gx', 'gy'))
Inputs may be any that keep to these rules, and one draw needn't show every extreme that they name: `well_cell`: no two tests pump at the same cell. `obs_test`: observation o names a test of group o // 96, that is one of tests (o // 96) * 32 to (o // 96 + 1) * 32 - 1; every test of a group is named by some observation of that group. `obs_pair`: observation o names a test of group o // 96, that is one of tests (o // 96) * 32 to (o // 96 + 1) * 32 - 1; every test of a group is named by some observation of that group.
All inputs are finite; a program needn't handle non-finite values.
Results may differ from a plain program's by a relative error of at most 0.0003.
Values may be sent and summed in bfloat16 or wider, within the bound.
A program may use at most 64 MiB of HBM per device.

v0:
```python
import jax
import jax.numpy as jnp
from jax import lax
from jax.sharding import PartitionSpec as P

ITERS = 2


STORAGE = 0.25
HIGHEST_PRECISION = lax.Precision.HIGHEST


def padded_2(x, sides, width):
    for axis, dim in sides:
        peers, length = (lax.axis_size(axis), x.shape[dim])
        up = [(i, (i + 1) % peers) for i in range(peers - 1)]
        down = [(j, i) for i, j in up]
        last = lax.slice_in_dim(x, length - width, length, axis=dim)
        leading = lax.slice_in_dim(x, 0, width, axis=dim)
        before = lax.ppermute(last, axis, up)
        after = lax.ppermute(leading, axis, down)
        x = jnp.concatenate([before, x, after], axis=dim)
    return x


def flat_rows(array_in):
    return array_in.reshape(array_in.shape[0], -1)


def gram_local(first_field, second_field):
    return jnp.dot(flat_rows(first_field), flat_rows(second_field).T, precision=HIGHEST_PRECISION)


def combine(coefficients, field_in):
    mixed_rows = jnp.dot(coefficients.T, flat_rows(field_in), precision=HIGHEST_PRECISION)
    return mixed_rows.reshape(field_in.shape)


def solve_spd(matrix, right_side):
    factor = jnp.linalg.cholesky(matrix)
    return jax.scipy.linalg.cho_solve((factor, True), right_side)


def layer_above(field_in):
    return jnp.concatenate([field_in[..., 1:], jnp.zeros_like(field_in[..., :1])], axis=-1)


def layer_below(field_in):
    return jnp.concatenate([jnp.zeros_like(field_in[..., :1]), field_in[..., :-1]], axis=-1)


def neighbour_views(padded, field_in):
    return (
        padded[:, 2:, 1:-1],
        padded[:, :-2, 1:-1],
        padded[:, 1:-1, 2:],
        padded[:, 1:-1, :-2],
        layer_above(field_in),
        layer_below(field_in),
    )


def pair_product(first_rows, second_rows):
    return lax.dot_general(
        first_rows, second_rows, (((1,), (1,)), ((), ())), preferred_element_type=jnp.float32
    )


def body(prior_heads, facies, facies_cond, well_cell, pump_rate, obs_test, obs_pair):
    group_size, rows_x, rows_y, layers = prior_heads.shape
    conduct = jnp.zeros(facies.shape, jnp.float32)
    for category in range(facies_cond.shape[0]):
        conduct = jnp.where(facies == category, facies_cond[category], conduct)
    cond_pad = padded_2(conduct, (("gx", 0), ("gy", 1)), 1)
    face_cond = [
        (conduct + neighbour[0]) * 0.5
        for neighbour in neighbour_views(cond_pad[None], conduct[None])
    ]
    diagonal = STORAGE + sum(face_cond)

    def padded_faces(field_in):
        return padded_2(field_in, (("gx", 1), ("gy", 2)), 1)

    def operate(field_in):
        result_field = diagonal * field_in
        for weight, neighbour in zip(face_cond, neighbour_views(padded_faces(field_in), field_in)):
            result_field = result_field - weight * neighbour
        return result_field

    size_y = rows_y * lax.axis_size("gy")
    pos_x = lax.axis_index("gx") * rows_x + lax.broadcasted_iota(jnp.int32, facies.shape, 0)
    pos_y = lax.axis_index("gy") * rows_y + lax.broadcasted_iota(jnp.int32, facies.shape, 1)
    pos_z = lax.broadcasted_iota(jnp.int32, facies.shape, 2)
    cell_ids = (pos_x * size_y + pos_y) * layers + pos_z
    source = jnp.where(
        cell_ids[None] == well_cell[:, None, None, None], -pump_rate[:, None, None, None], 0.0
    )
    head_field = prior_heads
    residual = source - operate(prior_heads)

    def reduced(first_field, second_field):
        return lax.psum(gram_local(first_field, second_field), ("gx", "gy"))

    direction = residual
    norm_now = reduced(residual, residual)
    for iteration in range(ITERS):
        applied = operate(direction)
        alpha_coef = solve_spd(reduced(direction, applied), norm_now)
        head_field = head_field + combine(alpha_coef, direction)
        residual = residual - combine(alpha_coef, applied)
        if iteration + 1 < ITERS:
            norm_next = reduced(residual, residual)
            beta_coef = solve_spd(norm_now, norm_next)
            direction = residual + combine(beta_coef, direction)
            norm_now = norm_next
    near_heads = neighbour_views(padded_faces(head_field), head_field)
    group_start = lax.axis_index("ta") * group_size
    first_local = obs_test - group_start
    second_local = obs_pair - group_start
    accumulated = jnp.zeros((obs_test.shape[0],) + facies.shape, jnp.float32)
    for direction_index in range(3):
        gradient = (near_heads[2 * direction_index] - near_heads[2 * direction_index + 1]) * 0.5
        accumulated = accumulated + jnp.take(gradient, first_local, axis=0) * jnp.take(
            gradient, second_local, axis=0
        )
    sensitivity = (-conduct * accumulated).astype(jnp.bfloat16).reshape(obs_test.shape[0], -1)
    partial_rows = pair_product(sensitivity, lax.all_gather(sensitivity, "ta", axis=0, tiled=True))
    summed = lax.psum_scatter(partial_rows, ("gx", "gy"), scatter_dimension=1, tiled=True)
    total_cells = rows_x * lax.axis_size("gx") * size_y * layers
    return (head_field, summed / float(total_cells))


def solution(mesh):
    in_specs = (
        P("ta", "gx", "gy", None),
        P("gx", "gy", None),
        P(),
        P("ta"),
        P("ta"),
        P("ta"),
        P("ta"),
    )
    out_specs = (P("ta", "gx", "gy", None), P("ta", ("gx", "gy")))
    return jax.shard_map(body, mesh=mesh, in_specs=in_specs, out_specs=out_specs, check_vma=False)
```

profile of v0, /device:TPU:0, one launch (start us, length us, event | category | flops | bytes accessed | tf_op | source)
XLA Modules:
  0.0 401.6 jit_solution(1570149263346726243)
XLA Ops:
  0.6 1.6 fusion.110
  2.2 0.7 copy-done.1
  2.9 3.8 fusion.92
  6.7 4.9 %collective-permute-start = (f32[1,8,128]{2,1,0:T(8,128)S(1)}, f32[1,8,128]{2,1,0:T(8,128)S(1)}, u32[]{:S(2)}, u32[]{:S(2)}) collective-permute-start(f32[1,8,128]{2,1,0:T(8,128)S(1)} %get-tuple-element.56), channel_id=1, source_target_pairs={{0,8},{8,16},{16,24},{1,9},{9,17},{17,25},{2,10},{10,18},{18,26},{... | collective-permute-start | bytes 12296 | tf_op jit(solution)/shard_map/ppermute | solution.py:20
  11.6 1.3 collective-permute-start.1
  12.9 1.0 copy.72
  14.0 4.6 %collective-permute-start.5 = (f32[32,1,8,128]{3,0,2,1:T(8,128)S(1)}, f32[32,1,8,128]{3,0,2,1:T(8,128)S(1)}, u32[]{:S(2)}, u32[]{:S(2)}) collective-permute-start(f32[32,1,8,128]{3,0,2,1:T(8,128)S(1)} %get-tuple-element.51), channel_id=1, source_target_pairs={{0,8},{8,16},{16,24},{1,9},{9,17},{17,25},{2,10},{10,18},{18,26},{... | collective-permute-start | bytes 393224 | tf_op jit(solution)/shard_map/ppermute | solution.py:20
  18.6 1.3 collective-permute-start.4
  20.6 3.4 collective-permute-start.2
  24.0 1.3 collective-permute-start.3
  25.4 4.1 %collective-permute-done.3 = f32[4,1,128]{2,1,0:T(1,128)S(1)} collective-permute-done((f32[4,1,128]{2,1,0:T(1,128)S(1)}, f32[4,1,128]{2,1,0:T(1,128)S(1)}, u32[]{:S(2)}, u32[]{:S(2)}) %collective-permute-start.3) | collective-permute-done | bytes 2080 | tf_op jit(solution)/shard_map/ppermute | solution.py:21
  29.7 1.3 collective-permute-start.6
  31.0 4.9 %collective-permute-start.7 = (f32[32,4,1,128]{3,0,2,1:T(8,128)S(1)}, f32[32,4,1,128]{3,0,2,1:T(8,128)S(1)}, u32[]{:S(2)}, u32[]{:S(2)}) collective-permute-start(f32[32,4,1,128]{3,0,2,1:T(8,128)S(1)} %get-tuple-element.35), channel_id=1, source_target_pairs={{0,2},{2,4},{4,6},{1,3},{3,5},{5,7},{8,10},{10,12},{12,14},{9,11},... | collective-permute-start | bytes 196616 | tf_op jit(solution)/shard_map/ppermute | solution.py:20
  36.2 1.6 collective-permute-done.7
  37.8 0.7 copy-done.2
  38.7 1.3 collective-permute-start.8
  40.0 5.2 %collective-permute-start.9 = (f32[32,1,8,128]{3,0,2,1:T(8,128)S(1)}, f32[32,1,8,128]{3,0,2,1:T(8,128)S(1)}, u32[]{:S(2)}, u32[]{:S(2)}) collective-permute-start(f32[32,1,8,128]{3,0,2,1:T(8,128)S(1)} %get-tuple-element.46), channel_id=1, source_target_pairs={{0,8},{8,16},{16,24},{1,9},{9,17},{17,25},{2,10},{10,18},{18,26},{... | collective-permute-start | bytes 393224 | tf_op jit(solution)/shard_map/ppermute | solution.py:20
  45.4 0.9 collective-permute-done.8
  46.2 1.5 collective-permute-done.9
  47.7 1.3 collective-permute-start.10
  49.0 5.4 %collective-permute-start.11 = (f32[32,4,1,128]{3,0,2,1:T(8,128)S(1)}, f32[32,4,1,128]{3,0,2,1:T(8,128)S(1)}, u32[]{:S(2)}, u32[]{:S(2)}) collective-permute-start(f32[32,4,1,128]{3,0,2,1:T(8,128)S(1)} %get-tuple-element.33), channel_id=1, source_target_pairs={{0,2},{2,4},{4,6},{1,3},{3,5},{5,7},{8,10},{10,12},{12,14},{9,11},... | collective-permute-start | bytes 196616 | tf_op jit(solution)/shard_map/ppermute | solution.py:20
  55.2 1.2 collective-permute-done.11
  57.1 81.6 %all-reduce.12 = (f32[32,32]{0,1:T(8,128)S(1)}, f32[32,32]{0,1:T(8,128)S(1)}) all-reduce(f32[32,32]{0,1:T(8,128)S(1)} %convolution_bitcast_fusion.5, f32[32,32]{0,1:T(8,128)S(1)} %convolution_bitcast_fusion.6), channel_id=1, replica_groups=mesh['gx'=4,'gy'=4,'ta'=2] {'gx','gy'}, use_global_device_ids=true, to_apply=%region_3.5 | all-reduce | flops 2048 | bytes 16384 | tf_op jit(solution)/shard_map/psum | solution.py:102
  138.9 2.9 cholesky.70
  141.8 0.6 compare_reduce_fusion.1
  142.4 0.7 fusion.65
  143.1 2.4 custom-call.10
  145.7 2.9 cholesky.59
  148.7 0.6 compare_reduce_fusion.2
  149.3 0.7 fusion.64
  150.0 2.4 custom-call.9
  153.6 71.7 %psum.30 = f32[32,32]{1,0:T(8,128)S(1)} all-reduce(f32[32,32]{1,0:T(8,128)S(1)} %convolution_bitcast_fusion.4), channel_id=1, replica_groups=mesh['gx'=4,'gy'=4,'ta'=2] {'gx','gy'}, use_global_device_ids=true, to_apply=%region_4.7 | all-reduce | flops 1024 | bytes 8192 | tf_op jit(solution)/shard_map/psum | solution.py:102
  226.3 1.3 collective-permute-start.12
  227.6 4.6 %collective-permute-start.13 = (f32[32,1,8,128]{3,0,2,1:T(8,128)S(1)}, f32[32,1,8,128]{3,0,2,1:T(8,128)S(1)}, u32[]{:S(2)}, u32[]{:S(2)}) collective-permute-start(f32[32,1,8,128]{3,0,2,1:T(8,128)S(1)} %get-tuple-element.42), channel_id=1, source_target_pairs={{0,8},{8,16},{16,24},{1,9},{9,17},{17,25},{2,10},{10,18},{18,26},{... | collective-permute-start | bytes 393224 | tf_op jit(solution)/shard_map/ppermute | solution.py:20
  233.1 1.5 collective-permute-done.13
  234.6 1.3 collective-permute-start.14
  235.9 4.5 %collective-permute-start.15 = (f32[32,4,1,128]{3,0,2,1:T(8,128)S(1)}, f32[32,4,1,128]{3,0,2,1:T(8,128)S(1)}, u32[]{:S(2)}, u32[]{:S(2)}) collective-permute-start(f32[32,4,1,128]{3,0,2,1:T(8,128)S(1)} %get-tuple-element.31), channel_id=1, source_target_pairs={{0,2},{2,4},{4,6},{1,3},{3,5},{5,7},{8,10},{10,12},{12,14},{9,11},... | collective-permute-start | bytes 196616 | tf_op jit(solution)/shard_map/ppermute | solution.py:20
  241.0 1.4 collective-permute-done.15
  242.9 74.0 %psum.31 = f32[32,32]{0,1:T(8,128)S(1)} all-reduce(f32[32,32]{0,1:T(8,128)S(1)} %convolution_bitcast_fusion.3), channel_id=1, replica_groups=mesh['gx'=4,'gy'=4,'ta'=2] {'gx','gy'}, use_global_device_ids=true, to_apply=%region_5.8 | all-reduce | flops 1024 | bytes 8192 | tf_op jit(solution)/shard_map/psum | solution.py:102
  316.9 2.9 cholesky.81
  319.9 0.6 compare_reduce_fusion
  320.5 0.7 fusion.66
  321.2 2.4 custom-call.11
  324.5 1.3 collective-permute-start.16
  325.8 4.6 %collective-permute-start.17 = (f32[32,1,8,128]{3,0,2,1:T(8,128)S(1)}, f32[32,1,8,128]{3,0,2,1:T(8,128)S(1)}, u32[]{:S(2)}, u32[]{:S(2)}) collective-permute-start(f32[32,1,8,128]{3,0,2,1:T(8,128)S(1)} %get-tuple-element.36), channel_id=1, source_target_pairs={{0,8},{8,16},{16,24},{1,9},{9,17},{17,25},{2,10},{10,18},{18,26},{... | collective-permute-start | bytes 393224 | tf_op jit(solution)/shard_map/ppermute | solution.py:20
  330.5 0.9 collective-permute-done.16
  331.4 1.5 collective-permute-done.17
  332.9 1.3 collective-permute-start.18
  334.2 4.5 %collective-permute-start.19 = (f32[32,4,1,128]{3,0,2,1:T(8,128)S(1)}, f32[32,4,1,128]{3,0,2,1:T(8,128)S(1)}, u32[]{:S(2)}, u32[]{:S(2)}) collective-permute-start(f32[32,4,1,128]{3,0,2,1:T(8,128)S(1)} %get-tuple-element.29), channel_id=1, source_target_pairs={{0,2},{2,4},{4,6},{1,3},{3,5},{5,7},{8,10},{10,12},{12,14},{9,11},... | collective-permute-start | bytes 196616 | tf_op jit(solution)/shard_map/ppermute | solution.py:20
  339.1 0.7 gather_fusion.4
  339.8 0.7 gather_fusion.5
  340.9 0.7 gather_fusion
  341.6 1.6 gather_fusion.1
  343.3 1.6 gather_fusion.2
  344.9 1.6 gather_fusion.3
  346.5 2.0 fusion.3
  348.7 2.4 all_gather.3
  351.4 40.2 %fusion = f32[96,16]{0,1:T(8,128)S(1)} fusion(f32[96,192]{0,1:T(8,128)S(1)} %fusion.91), kind=kCustom, calls=%all-reduce-scatter | all-reduce-scatter fusion | flops 24577 | bytes 80384
  391.6 2.3 collective-permute-start.20
  393.9 1.3 collective-permute-start.21
  395.2 1.3 collective-permute-start.22
  396.5 1.9 collective-permute-start.23
  399.7 0.9 copy.90
  401.0 0.6 dynamic-slice_multiply_fusion
  (97 shorter events, 10.8 us)
Async XLA Ops:
  2.2 0.7 copy-start.1
  6.7 13.9 %collective-permute-start = (f32[1,8,128]{2,1,0:T(8,128)S(1)}, f32[1,8,128]{2,1,0:T(8,128)S(1)}, u32[]{:S(2)}, u32[]{:S(2)}) collective-permute-start(f32[1,8,128]{2,1,0:T(8,128)S(1)} %get-tuple-element.56), channel_id=1, source_target_pairs={{0,8},{8,16},{16,24},{1,9},{9,17},{17,25},{2,10},{10,18},{18,26},{... | collective-permute-start | bytes 12296 | tf_op jit(solution)/shard_map/ppermute | solution.py:20
  11.6 8.9 %collective-permute-start.1 = (f32[1,8,128]{2,1,0:T(8,128)S(1)}, f32[1,8,128]{2,1,0:T(8,128)S(1)}, u32[]{:S(2)}, u32[]{:S(2)}) collective-permute-start(f32[1,8,128]{2,1,0:T(8,128)S(1)} %get-tuple-element.57), channel_id=1, source_target_pairs={{8,0},{16,8},{24,16},{9,1},{17,9},{25,17},{10,2},{18,10},{26,18},{... | collective-permute-start | bytes 12296 | tf_op jit(solution)/shard_map/ppermute | solution.py:21
  14.0 15.5 %collective-permute-start.5 = (f32[32,1,8,128]{3,0,2,1:T(8,128)S(1)}, f32[32,1,8,128]{3,0,2,1:T(8,128)S(1)}, u32[]{:S(2)}, u32[]{:S(2)}) collective-permute-start(f32[32,1,8,128]{3,0,2,1:T(8,128)S(1)} %get-tuple-element.51), channel_id=1, source_target_pairs={{0,8},{8,16},{16,24},{1,9},{9,17},{17,25},{2,10},{10,18},{18,26},{... | collective-permute-start | bytes 393224 | tf_op jit(solution)/shard_map/ppermute | solution.py:20
  18.6 11.1 %collective-permute-start.4 = (f32[32,1,8,128]{3,0,2,1:T(8,128)S(1)}, f32[32,1,8,128]{3,0,2,1:T(8,128)S(1)}, u32[]{:S(2)}, u32[]{:S(2)}) collective-permute-start(f32[32,1,8,128]{3,0,2,1:T(8,128)S(1)} %get-tuple-element.50), channel_id=1, source_target_pairs={{8,0},{16,8},{24,16},{9,1},{17,9},{25,17},{10,2},{18,10},{26,18},{... | collective-permute-start | bytes 393224 | tf_op jit(solution)/shard_map/ppermute | solution.py:21
  19.9 0.7 copy-start.3
  19.9 0.7 copy-start.4
  19.9 5.4 %copy-start.6 = (f32[32]{0:T(128)S(1)}, f32[32]{0:T(128)}, u32[]{:S(2)}) copy-start(f32[32]{0:T(128)} %param.16) | copy-start | bytes 388
  20.1 9.5 %copy-start = (f32[32,2,8,128]{3,2,1,0:T(8,128)S(1)}, f32[32,2,8,128]{3,2,1,0:T(8,128)}, u32[]{:S(2)}) copy-start(f32[32,2,8,128]{3,2,1,0:T(8,128)} %param.12) | copy-start | bytes 786436
  20.6 4.7 %collective-permute-start.2 = (f32[4,1,128]{2,1,0:T(1,128)S(1)}, f32[4,1,128]{2,1,0:T(1,128)S(1)}, u32[]{:S(2)}, u32[]{:S(2)}) collective-permute-start(f32[4,1,128]{2,1,0:T(1,128)S(1)} %get-tuple-element.52), channel_id=1, source_target_pairs={{0,2},{2,4},{4,6},{1,3},{3,5},{5,7},{8,10},{10,12},{12,14},{9,11},... | collective-permute-start | bytes 6152 | tf_op jit(solution)/shard_map/ppermute | solution.py:20
  24.0 5.5 %collective-permute-start.3 = (f32[4,1,128]{2,1,0:T(1,128)S(1)}, f32[4,1,128]{2,1,0:T(1,128)S(1)}, u32[]{:S(2)}, u32[]{:S(2)}) collective-permute-start(f32[4,1,128]{2,1,0:T(1,128)S(1)} %get-tuple-element.53), channel_id=1, source_target_pairs={{2,0},{4,2},{6,4},{3,1},{5,3},{7,5},{10,8},{12,10},{14,12},{11,9},... | collective-permute-start | bytes 6152 | tf_op jit(solution)/shard_map/ppermute | solution.py:21
  29.7 6.5 %collective-permute-start.6 = (f32[32,4,1,128]{3,0,2,1:T(8,128)S(1)}, f32[32,4,1,128]{3,0,2,1:T(8,128)S(1)}, u32[]{:S(2)}, u32[]{:S(2)}) collective-permute-start(f32[32,4,1,128]{3,0,2,1:T(8,128)S(1)} %get-tuple-element.34), channel_id=1, source_target_pairs={{2,0},{4,2},{6,4},{3,1},{5,3},{7,5},{10,8},{12,10},{14,12},{11,9},... | collective-permute-start | bytes 196616 | tf_op jit(solution)/shard_map/ppermute | solution.py:21
  31.0 6.8 %collective-permute-start.7 = (f32[32,4,1,128]{3,0,2,1:T(8,128)S(1)}, f32[32,4,1,128]{3,0,2,1:T(8,128)S(1)}, u32[]{:S(2)}, u32[]{:S(2)}) collective-permute-start(f32[32,4,1,128]{3,0,2,1:T(8,128)S(1)} %get-tuple-element.35), channel_id=1, source_target_pairs={{0,2},{2,4},{4,6},{1,3},{3,5},{5,7},{8,10},{10,12},{12,14},{9,11},... | collective-permute-start | bytes 196616 | tf_op jit(solution)/shard_map/ppermute | solution.py:20
  37.8 0.7 copy-start.2
  38.7 7.5 %collective-permute-start.8 = (f32[32,1,8,128]{3,0,2,1:T(8,128)S(1)}, f32[32,1,8,128]{3,0,2,1:T(8,128)S(1)}, u32[]{:S(2)}, u32[]{:S(2)}) collective-permute-start(f32[32,1,8,128]{3,0,2,1:T(8,128)S(1)} %get-tuple-element.47), channel_id=1, source_target_pairs={{8,0},{16,8},{24,16},{9,1},{17,9},{25,17},{10,2},{18,10},{26,18},{... | collective-permute-start | bytes 393224 | tf_op jit(solution)/shard_map/ppermute | solution.py:21
  40.0 7.7 %collective-permute-start.9 = (f32[32,1,8,128]{3,0,2,1:T(8,128)S(1)}, f32[32,1,8,128]{3,0,2,1:T(8,128)S(1)}, u32[]{:S(2)}, u32[]{:S(2)}) collective-permute-start(f32[32,1,8,128]{3,0,2,1:T(8,128)S(1)} %get-tuple-element.46), channel_id=1, source_target_pairs={{0,8},{8,16},{16,24},{1,9},{9,17},{17,25},{2,10},{10,18},{18,26},{... | collective-permute-start | bytes 393224 | tf_op jit(solution)/shard_map/ppermute | solution.py:20
  47.7 7.4 %collective-permute-start.10 = (f32[32,4,1,128]{3,0,2,1:T(8,128)S(1)}, f32[32,4,1,128]{3,0,2,1:T(8,128)S(1)}, u32[]{:S(2)}, u32[]{:S(2)}) collective-permute-start(f32[32,4,1,128]{3,0,2,1:T(8,128)S(1)} %get-tuple-element.32), channel_id=1, source_target_pairs={{2,0},{4,2},{6,4},{3,1},{5,3},{7,5},{10,8},{12,10},{14,12},{11,9},... | collective-permute-start | bytes 196616 | tf_op jit(solution)/shard_map/ppermute | solution.py:21
  49.0 7.3 %collective-permute-start.11 = (f32[32,4,1,128]{3,0,2,1:T(8,128)S(1)}, f32[32,4,1,128]{3,0,2,1:T(8,128)S(1)}, u32[]{:S(2)}, u32[]{:S(2)}) collective-permute-start(f32[32,4,1,128]{3,0,2,1:T(8,128)S(1)} %get-tuple-element.33), channel_id=1, source_target_pairs={{0,2},{2,4},{4,6},{1,3},{3,5},{5,7},{8,10},{10,12},{12,14},{9,11},... | collective-permute-start | bytes 196616 | tf_op jit(solution)/shard_map/ppermute | solution.py:20
  226.3 6.9 %collective-permute-start.12 = (f32[32,1,8,128]{3,0,2,1:T(8,128)S(1)}, f32[32,1,8,128]{3,0,2,1:T(8,128)S(1)}, u32[]{:S(2)}, u32[]{:S(2)}) collective-permute-start(f32[32,1,8,128]{3,0,2,1:T(8,128)S(1)} %get-tuple-element.43), channel_id=1, source_target_pairs={{8,0},{16,8},{24,16},{9,1},{17,9},{25,17},{10,2},{18,10},{26,18},{... | collective-permute-start | bytes 393224 | tf_op jit(solution)/shard_map/ppermute | solution.py:21
  227.6 7.1 %collective-permute-start.13 = (f32[32,1,8,128]{3,0,2,1:T(8,128)S(1)}, f32[32,1,8,128]{3,0,2,1:T(8,128)S(1)}, u32[]{:S(2)}, u32[]{:S(2)}) collective-permute-start(f32[32,1,8,128]{3,0,2,1:T(8,128)S(1)} %get-tuple-element.42), channel_id=1, source_target_pairs={{0,8},{8,16},{16,24},{1,9},{9,17},{17,25},{2,10},{10,18},{18,26},{... | collective-permute-start | bytes 393224 | tf_op jit(solution)/shard_map/ppermute | solution.py:20
  234.6 6.3 %collective-permute-start.14 = (f32[32,4,1,128]{3,0,2,1:T(8,128)S(1)}, f32[32,4,1,128]{3,0,2,1:T(8,128)S(1)}, u32[]{:S(2)}, u32[]{:S(2)}) collective-permute-start(f32[32,4,1,128]{3,0,2,1:T(8,128)S(1)} %get-tuple-element.30), channel_id=1, source_target_pairs={{2,0},{4,2},{6,4},{3,1},{5,3},{7,5},{10,8},{12,10},{14,12},{11,9},... | collective-permute-start | bytes 196616 | tf_op jit(solution)/shard_map/ppermute | solution.py:21
  235.9 6.4 %collective-permute-start.15 = (f32[32,4,1,128]{3,0,2,1:T(8,128)S(1)}, f32[32,4,1,128]{3,0,2,1:T(8,128)S(1)}, u32[]{:S(2)}, u32[]{:S(2)}) collective-permute-start(f32[32,4,1,128]{3,0,2,1:T(8,128)S(1)} %get-tuple-element.31), channel_id=1, source_target_pairs={{0,2},{2,4},{4,6},{1,3},{3,5},{5,7},{8,10},{10,12},{12,14},{9,11},... | collective-permute-start | bytes 196616 | tf_op jit(solution)/shard_map/ppermute | solution.py:20
  324.5 6.9 %collective-permute-start.16 = (f32[32,1,8,128]{3,0,2,1:T(8,128)S(1)}, f32[32,1,8,128]{3,0,2,1:T(8,128)S(1)}, u32[]{:S(2)}, u32[]{:S(2)}) collective-permute-start(f32[32,1,8,128]{3,0,2,1:T(8,128)S(1)} %get-tuple-element.37), channel_id=1, source_target_pairs={{8,0},{16,8},{24,16},{9,1},{17,9},{25,17},{10,2},{18,10},{26,18},{... | collective-permute-start | bytes 393224 | tf_op jit(solution)/shard_map/ppermute | solution.py:21
  325.8 7.1 %collective-permute-start.17 = (f32[32,1,8,128]{3,0,2,1:T(8,128)S(1)}, f32[32,1,8,128]{3,0,2,1:T(8,128)S(1)}, u32[]{:S(2)}, u32[]{:S(2)}) collective-permute-start(f32[32,1,8,128]{3,0,2,1:T(8,128)S(1)} %get-tuple-element.36), channel_id=1, source_target_pairs={{0,8},{8,16},{16,24},{1,9},{9,17},{17,25},{2,10},{10,18},{18,26},{... | collective-permute-start | bytes 393224 | tf_op jit(solution)/shard_map/ppermute | solution.py:20
  332.9 7.6 %collective-permute-start.18 = (f32[32,4,1,128]{3,0,2,1:T(8,128)S(1)}, f32[32,4,1,128]{3,0,2,1:T(8,128)S(1)}, u32[]{:S(2)}, u32[]{:S(2)}) collective-permute-start(f32[32,4,1,128]{3,0,2,1:T(8,128)S(1)} %get-tuple-element.28), channel_id=1, source_target_pairs={{2,0},{4,2},{6,4},{3,1},{5,3},{7,5},{10,8},{12,10},{14,12},{11,9},... | collective-permute-start | bytes 196616 | tf_op jit(solution)/shard_map/ppermute | solution.py:21
  334.2 6.4 %collective-permute-start.19 = (f32[32,4,1,128]{3,0,2,1:T(8,128)S(1)}, f32[32,4,1,128]{3,0,2,1:T(8,128)S(1)}, u32[]{:S(2)}, u32[]{:S(2)}) collective-permute-start(f32[32,4,1,128]{3,0,2,1:T(8,128)S(1)} %get-tuple-element.29), channel_id=1, source_target_pairs={{0,2},{2,4},{4,6},{1,3},{3,5},{5,7},{8,10},{10,12},{12,14},{9,11},... | collective-permute-start | bytes 196616 | tf_op jit(solution)/shard_map/ppermute | solution.py:20
  391.6 8.9 %collective-permute-start.20 = (f32[96,16]{0,1:T(8,128)S(1)}, f32[96,16]{0,1:T(8,128)S(1)}, u32[]{:S(2)}, u32[]{:S(2)}) collective-permute-start(f32[96,16]{0,1:T(8,128)S(1)} %fusion), channel_id=1, source_target_pairs={{0,2},{2,4},{4,6},{6,8},{8,10},{10,12},{12,14},{14,16},{16,18},{18... | collective-permute-start | bytes 18440
  393.9 6.6 %collective-permute-start.21 = (f32[96,16]{0,1:T(8,128)S(1)}, f32[96,16]{0,1:T(8,128)S(1)}, u32[]{:S(2)}, u32[]{:S(2)}) collective-permute-start(f32[96,16]{0,1:T(8,128)S(1)} %fusion), channel_id=1, source_target_pairs={{0,4},{2,6},{4,8},{6,10},{8,12},{10,14},{12,16},{14,18},{16,20},{1... | collective-permute-start | bytes 18440
  395.2 5.3 %collective-permute-start.22 = (f32[96,16]{0,1:T(8,128)S(1)}, f32[96,16]{0,1:T(8,128)S(1)}, u32[]{:S(2)}, u32[]{:S(2)}) collective-permute-start(f32[96,16]{0,1:T(8,128)S(1)} %fusion), channel_id=1, source_target_pairs={{0,6},{2,8},{4,10},{6,12},{8,14},{10,16},{12,18},{14,20},{16,22},{... | collective-permute-start | bytes 18440
  396.5 1.9 copy-start.5
  396.5 4.0 collective-permute-start.23
where the time goes:
time: 403 us; the launch traced here: 402 us
  blocking collectives  270 us (67%)
  starting transfers between devices  66.3 us (16%)
  other arithmetic  27.4 us (7%)
  local copies, waits for them, and re-layouts  15.5 us (4%)
  waiting for transfers between devices  15.5 us (4%)
  matrix products  4.96 us (1%)
    psum x3, blocking collectives, reduced(): return lax.psum(gram_local(first_field, second_field), ('gx', 'gy'))  227 us
    ppermute x10, starting transfers between devices, padded_2(): before = lax.ppermute(last, axis, up)  46.6 us
    unnamed x1, blocking collectives  40.2 us
    ppermute x10, starting transfers between devices, padded_2(): after = lax.ppermute(leading, axis, down)  12.9 us
    another operation x9, other arithmetic, solve_spd(): factor = jnp.linalg.cholesky(matrix)  10.8 us
    another operation x6, other arithmetic, solve_spd(): return jax.scipy.linalg.cho_solve((factor, True), right_side)  9.26 us
    ppermute x10, waiting for transfers between devices, padded_2(): before = lax.ppermute(last, axis, up)  8.87 us
  transfers between devices with their start and end apart: 24, of which 12 were waited for; matrix products, arithmetic and copies ran while one was open for 2% of the time, Pallas kernels for 0%

commit v1 on v0

v1 whole, which is shorter than its diff:
```python
import functools

import jax
import jax.numpy as jnp
from jax import lax
from jax.experimental import pallas as pl
from jax.experimental.pallas import tpu as pltpu
from jax.sharding import PartitionSpec as P

STORAGE = 0.25
SCALE = 1.0 / 32.0
F32 = jnp.float32
BF16 = jnp.bfloat16
HIGHEST = lax.Precision.HIGHEST
CHUNKS = 4
PAD = 16
NT = (((1,), (1,)), ((), ()))
NN = (((1,), (0,)), ((), ()))


def split(value):
    high = value.astype(BF16)
    return high, (value - high.astype(F32)).astype(BF16)


def eliminate(table, first_lane, size):
    rows = lax.broadcasted_iota(jnp.int32, table.shape, 0)
    for k in range(size):
        lane = first_lane + k
        column = table[:, lane:lane + 1]
        pivot = table[k:k + 1, lane:lane + 1]
        scaled = table[k:k + 1, :] * (1.0 / pivot)
        table = jnp.where(rows == k, scaled, table - column * scaled)
    return table


def kernel(
    dims,
    prior, facies, facies_cond, well, rate, obs_test, obs_pair,
    heads, jjt,
    cond, cond_x, cond_y, cond_ys, weights,
    head_f, head_x, head_y,
    res_f, res_x, res_y,
    app_f, app_b, app_x, app_y, app_l,
    twice_f,
    res_h, res_l, res_xh, res_xl, res_yh, res_yl,
    fin_f, fin_x, fin_y,
    pick, sens, partial, part_y, part_x,
    sum_ax, sum_ay, sum_bx, sum_by,
    halo_send, halo_recv,
    ax_send, ax_recv, ay_send, ay_recv,
    rx_send, rx_recv, ry_send, ry_recv,
    ta_send, ta_recv,
):
    n_gx, n_gy, n_ta, group, rows_x, rows_y, layers, obs = dims
    gx, gy, ta = lax.axis_index("gx"), lax.axis_index("gy"), lax.axis_index("ta")
    cells = rows_x * rows_y
    size_y = rows_y * n_gy
    blocks = [(x, y) for x in range(rows_x) for y in range(rows_y)]
    owned = n_ta * obs // (n_gx * n_gy)
    owners = obs // owned
    padded = owners * PAD

    barrier = pltpu.get_barrier_semaphore()
    for axis, own, count in (("gx", gx, n_gx), ("gy", gy, n_gy), ("ta", ta, n_ta)):
        for step in range(1, count):
            pl.semaphore_signal(
                barrier, inc=1, device_id={axis: lax.rem(own + step, count)},
                device_id_type=pl.DeviceIdType.MESH,
            )

    def send(src, dst, send_sem, recv_sem, axis, peer):
        return pltpu.make_async_remote_copy(
            src_ref=src, dst_ref=dst, send_sem=send_sem, recv_sem=recv_sem,
            device_id={axis: peer}, device_id_type=pl.DeviceIdType.MESH,
        )

    up_x, down_x = lax.rem(gx + 1, n_gx), lax.rem(gx + n_gx - 1, n_gx)
    up_y, down_y = lax.rem(gy + 1, n_gy), lax.rem(gy + n_gy - 1, n_gy)
    lows = (gx > 0, gx < n_gx - 1, gy > 0, gy < n_gy - 1)
    outs = (gx < n_gx - 1, gx > 0, gy < n_gy - 1, gy > 0)

    def exchange(stage, sources, halo_x, halo_y):
        places = (halo_x.at[0], halo_x.at[1], halo_y.at[0], halo_y.at[1])
        axes = ("gx", "gx", "gy", "gy")
        peers = (up_x, down_x, up_y, down_y)
        return [
            send(src, dst, halo_send.at[stage, i], halo_recv.at[stage, i], axes[i], peers[i])
            for i, (src, dst) in enumerate(zip(sources, places))
        ]

    def start(copies):
        for copy, out in zip(copies, outs):
            pl.when(out)(copy.start)

    def arrived(copies):
        for copy, low in zip(copies, lows):
            pl.when(low)(copy.wait_recv)

    def sent(copies):
        for copy, out in zip(copies, outs):
            pl.when(out)(copy.wait_send)

    def faces(field):
        return (field.at[rows_x - 1], field.at[0], field.at[:, rows_y - 1], field.at[:, 0])

    kinds = facies[...]
    conduct = jnp.zeros(kinds.shape, F32)
    mean = jnp.float32(0.0)
    for c in range(facies_cond.shape[0]):
        conduct = jnp.where(kinds == c, facies_cond[c], conduct)
        mean = mean + facies_cond[c]
    cond[...] = conduct
    cond_ys[...] = jnp.zeros(cond_ys.shape, F32)
    for x in range(rows_x):
        cond_ys[0, x:x + 1, :] = conduct[(x + 1) * rows_y - 1:(x + 1) * rows_y]
        cond_ys[1, x:x + 1, :] = conduct[x * rows_y:x * rows_y + 1]
    shift = STORAGE + mean * (9.0 / facies_cond.shape[0])
    for x, y in blocks:
        head_f[x, y] = prior[pl.ds(x * rows_y + y, group, stride=cells), :]
    for side, low in enumerate(lows):
        @pl.when(jnp.logical_not(low))
        def _():
            for halo in ((cond_x, head_x, res_x, app_x) if side < 2 else (cond_y, head_y, res_y, app_y)):
                halo[side % 2] = jnp.zeros(halo.shape[1:], halo.dtype)

    pl.semaphore_wait(barrier, n_gx + n_gy + n_ta - 3)
    first_rows, last_rows = pl.ds(0, rows_y), pl.ds((rows_x - 1) * rows_y, rows_y)
    cond_copies = exchange(
        3, (cond.at[last_rows], cond.at[first_rows], cond_ys.at[0], cond_ys.at[1]), cond_x, cond_y
    )
    head_copies = exchange(0, faces(head_f), head_x, head_y)
    start(cond_copies)
    start(head_copies)

    lanes = lax.broadcasted_iota(jnp.int32, (group, layers), 1)
    tests = lax.broadcasted_iota(jnp.int32, (group, layers), 0)
    wells = jnp.zeros((group, layers), jnp.int32)
    rates = jnp.zeros((group, layers), F32)
    for t in range(group):
        wells = jnp.where(tests == t, well[t], wells)
        rates = jnp.where(tests == t, -rate[t], rates)
    wells = wells - lanes

    pad_rows = lax.broadcasted_iota(jnp.int32, (PAD, 128), 0)
    pad_lanes = lax.broadcasted_iota(jnp.int32, (PAD, 128), 1)
    slot = jnp.where(pad_lanes < 2 * group, lax.rem(pad_lanes, group), -2)
    for half, table in enumerate((obs_test, obs_pair)):
        for k in range(owners):
            named = jnp.full((PAD, 128), -1, jnp.int32)
            for j in range(owned):
                named = jnp.where(pad_rows == j, table[k * owned + j] - ta * group, named)
            pick[pl.ds(half * padded + k * PAD, PAD), :] = jnp.where(named == slot, 1.0, 0.0).astype(BF16)

    arrived(cond_copies)
    one_lane = lax.broadcasted_iota(jnp.int32, (1, layers), 1)
    for x, y in blocks:
        r = x * rows_y + y
        here = cond[r:r + 1, :]
        x_up = cond[r + rows_y:r + rows_y + 1, :] if x + 1 < rows_x else cond_x[1, y:y + 1, :]
        x_down = cond[r - rows_y:r - rows_y + 1, :] if x > 0 else cond_x[0, y:y + 1, :]
        y_up = cond[r + 1:r + 2, :] if y + 1 < rows_y else cond_y[1, x:x + 1, :]
        y_down = cond[r - 1:r, :] if y > 0 else cond_y[0, x:x + 1, :]
        z_up = jnp.where(one_lane < layers - 1, pltpu.roll(here, layers - 1, 1), 0.0)
        z_down = jnp.where(one_lane > 0, pltpu.roll(here, 1, 1), 0.0)
        face = [(here + other) * 0.5 for other in (x_up, x_down, y_up, y_down, z_up, z_down)]
        diagonal = STORAGE + sum(face)
        face[4] = jnp.where(one_lane < layers - 1, face[4], 0.0)
        face[5] = jnp.where(one_lane > 0, face[5], 0.0)
        for i, weight in enumerate(face):
            weights[i, r:r + 1, :] = weight
            weights[6 + i, r:r + 1, :] = weight * SCALE
        weights[12, r:r + 1, :] = diagonal
        weights[13, r:r + 1, :] = (diagonal - shift) * SCALE
        weights[14, r:r + 1, :] = diagonal * SCALE

    def weight(i, x, y):
        return weights[i, pl.ds(x * rows_y + y, 1), :]

    def inner(field, base, diag, x, y):
        here = field[x, y]
        total = weight(diag, x, y) * here
        if x + 1 < rows_x:
            total = total - weight(base, x, y) * field[x + 1, y]
        if x > 0:
            total = total - weight(base + 1, x, y) * field[x - 1, y]
        if y + 1 < rows_y:
            total = total - weight(base + 2, x, y) * field[x, y + 1]
        if y > 0:
            total = total - weight(base + 3, x, y) * field[x, y - 1]
        total = total - weight(base + 4, x, y) * pltpu.roll(here, layers - 1, 1)
        return total - weight(base + 5, x, y) * pltpu.roll(here, 1, 1)

    def outer(halo_x, halo_y, base, x, y):
        total = None
        terms = []
        if x == rows_x - 1:
            terms.append(weight(base, x, y) * halo_x[1, y].astype(F32))
        if x == 0:
            terms.append(weight(base + 1, x, y) * halo_x[0, y].astype(F32))
        if y == rows_y - 1:
            terms.append(weight(base + 2, x, y) * halo_y[1, x].astype(F32))
        if y == 0:
            terms.append(weight(base + 3, x, y) * halo_y[0, x].astype(F32))
        return sum(terms) if terms else None

    for x, y in blocks:
        cell = ((gx * rows_x + x) * size_y + gy * rows_y + y) * layers
        source = jnp.where(wells == cell, rates, 0.0)
        res_f[x, y] = source - inner(head_f, 0, 12, x, y)
    arrived(head_copies)
    for x, y in blocks:
        more = outer(head_x, head_y, 0, x, y)
        if more is not None:
            res_f[x, y] = res_f[x, y] + more
    res_copies = exchange(1, faces(res_f), res_x, res_y)
    start(res_copies)

    for x, y in blocks:
        app_f[x, y] = inner(res_f, 6, 13, x, y)
        res_h[x, y], res_l[x, y] = split(res_f[x, y])
    arrived(res_copies)
    for x, y in blocks:
        more = outer(res_x, res_y, 6, x, y)
        value = app_f[x, y]
        if more is not None:
            value = value - more
            app_f[x, y] = value
        app_b[x, y], app_l[x, y] = split(value)
    app_copies = exchange(2, faces(app_b), app_x, app_y)
    start(app_copies)

    stacked = jnp.concatenate(
        [
            jnp.concatenate([res_h[x, y], app_b[x, y], res_l[x, y], app_l[x, y]], axis=0)
            for x, y in blocks
        ],
        axis=1,
    )
    gram = lax.dot_general(stacked, stacked, NT, preferred_element_type=F32)
    gram = gram[:2 * group] + gram[2 * group:]
    gram = gram + pltpu.roll(gram, 2 * group, 1)
    table_lane = lax.broadcasted_iota(jnp.int32, (group, 4 * group), 1)

    def reduce_start(buffer, value, axis, own, count, sends, recvs):
        buffer[own] = value
        copies = []
        for step in range(1, count):
            peer = lax.rem(own + step, count)
            copies.append(send(buffer.at[own], buffer.at[own], sends.at[step], recvs.at[step], axis, peer))
            copies[-1].start()
        return copies

    def reduce_end(buffer, copies, count):
        for copy in copies:
            copy.wait_recv()
        total = buffer[0]
        for i in range(1, count):
            total = total + buffer[i]
        return total

    a_gx = reduce_start(
        sum_ax, jnp.where(table_lane < 2 * group, gram[:group], gram[group:]),
        "gx", gx, n_gx, ax_send.at[0], ax_recv.at[0],
    )
    for side in range(2):
        for y in range(rows_y):
            res_xh[side, y], res_xl[side, y] = split(res_x[side, y])
        for x in range(rows_x):
            res_yh[side, x], res_yl[side, x] = split(res_y[side, x])
    for x, y in blocks:
        twice_f[x, y] = inner(app_f, 6, 14, x, y)
    left = jnp.concatenate(
        [jnp.concatenate([app_b[x, y], app_l[x, y]], axis=0) for x, y in blocks], axis=1
    )
    arrived(app_copies)
    right = []
    for x, y in blocks:
        more = outer(app_x, app_y, 6, x, y)
        value = twice_f[x, y]
        high, low = split(value if more is None else value - more)
        right.append(jnp.concatenate([high, high, low, low], axis=0))
    gram = lax.dot_general(left, jnp.concatenate(right, axis=1), NT, preferred_element_type=F32)
    gram = gram[:group] + gram[group:]
    gram = gram + pltpu.roll(gram, 2 * group, 1)
    b_gx = reduce_start(sum_bx, gram, "gx", gx, n_gx, ax_send.at[1], ax_recv.at[1])
    total = reduce_end(sum_ax, a_gx, n_gx)
    a_gy = reduce_start(sum_ay, total, "gy", gy, n_gy, ay_send.at[0], ay_recv.at[0])
    total = reduce_end(sum_bx, b_gx, n_gx)
    b_gy = reduce_start(sum_by, total, "gy", gy, n_gy, ay_send.at[1], ay_recv.at[1])
    first = reduce_end(sum_ay, a_gy, n_gy)

    before = first + (shift * SCALE) * pltpu.roll(first, group, 1)
    before = jnp.where(table_lane < group, first, before)
    after = eliminate(before, group, group)
    keep = table_lane >= 3 * group
    gap = jnp.zeros((3 * group, 4 * group), F32)
    product = lax.dot_general(
        jnp.where(keep, before, 0.0), jnp.concatenate([gap, after], axis=0), NN,
        precision=HIGHEST, preferred_element_type=F32,
    )
    side = pltpu.roll(first, 3 * group, 1)
    second = reduce_end(sum_by, b_gy, n_gy)
    lower = eliminate(jnp.where(table_lane < group, side, second) - product, 3 * group, group)
    upper = after - lax.dot_general(
        jnp.where(keep, after, 0.0), jnp.concatenate([gap, lower], axis=0), NN,
        precision=HIGHEST, preferred_element_type=F32,
    )
    coef = jnp.concatenate([upper, lower, upper, lower], axis=0).T[:group] * SCALE
    coef_high, coef_low = split(coef)
    coef = jnp.concatenate([coef_high, coef_low], axis=0)

    def combined(bases, fields):
        right = jnp.concatenate([jnp.concatenate(parts, axis=0) for parts in fields], axis=1)
        change = lax.dot_general(coef, right, NN, preferred_element_type=F32)
        change = change[:group] + change[group:]
        return [base + change[:, i * layers:(i + 1) * layers] for i, base in enumerate(bases)]

    nothing = jnp.zeros((group, layers), BF16)
    work = []
    for x, y in blocks:
        work.append((fin_f, x, y, head_f, (res_h, app_b, res_l, app_l)))
    for s in range(2):
        for y in range(rows_y):
            work.append((fin_x, s, y, head_x, (res_xh, app_x, res_xl, None)))
        for x in range(rows_x):
            work.append((fin_y, s, x, head_y, (res_yh, app_y, res_yl, None)))
    for i in range(0, len(work), 2):
        pair = work[i:i + 2]
        results = combined(
            [base[a, b] for _, a, b, base, _ in pair],
            [[nothing if f is None else f[a, b] for f in parts] for _, a, b, _, parts in pair],
        )
        for (place, a, b, _, _), value in zip(pair, results):
            place[a, b] = value
            if place is fin_f:
                heads[pl.ds(a * rows_y + b, group, stride=cells), :] = value

    chosen = pick[:, :2 * group]
    per_chunk = cells // CHUNKS
    sens_copies = []
    for chunk in range(CHUNKS):
        for pos in range(0, per_chunk, 2):
            gradients = [[], [], []]
            conducts = []
            for x, y in blocks[chunk * per_chunk + pos:chunk * per_chunk + pos + 2]:
                here = fin_f[x, y]
                x_up = fin_f[x + 1, y] if x + 1 < rows_x else fin_x[1, y]
                x_down = fin_f[x - 1, y] if x > 0 else fin_x[0, y]
                y_up = fin_f[x, y + 1] if y + 1 < rows_y else fin_y[1, x]
                y_down = fin_f[x, y - 1] if y > 0 else fin_y[0, x]
                z_up = jnp.where(lanes < layers - 1, pltpu.roll(here, layers - 1, 1), 0.0)
                z_down = jnp.where(lanes > 0, pltpu.roll(here, 1, 1), 0.0)
                for d, (a, b) in enumerate(((x_up, x_down), (y_up, y_down), (z_up, z_down))):
                    gradients[d].append(jnp.concatenate(split((a - b) * 0.5), axis=0))
                r = x * rows_y + y
                conducts.append(cond[r:r + 1, :])
            total = None
            for d in range(3):
                taken = lax.dot_general(
                    chosen, jnp.concatenate(gradients[d], axis=1), NN, preferred_element_type=F32
                )
                term = taken[:padded] * taken[padded:]
                total = term if total is None else total + term
            value = (-jnp.concatenate(conducts, axis=1) * total).astype(BF16)
            sens[ta, chunk, :, pos * layers:(pos + 2) * layers] = value
        for step in range(1, n_ta):
            copy = send(
                sens.at[ta, chunk], sens.at[ta, chunk], ta_send.at[step, chunk],
                ta_recv.at[step, chunk], "ta", lax.rem(ta + step, n_ta),
            )
            copy.start()
            sens_copies.append((step, copy))

    def gathered(index):
        return jnp.concatenate([sens[index, chunk] for chunk in range(CHUNKS)], axis=1)

    for step in range(n_ta):
        for owner_step, copy in sens_copies:
            if owner_step == step:
                copy.wait_recv()
        index = lax.rem(ta + n_ta - step, n_ta)
        value = lax.dot_general(gathered(index), gathered(ta), NT, preferred_element_type=F32)
        for k in range(owners):
            b = index * owners + k
            partial[b // n_gy, lax.rem(b, n_gy)] = value[k * PAD:(k + 1) * PAD]

    y_copies = []
    for step in range(1, n_gy):
        peer = lax.rem(gy + step, n_gy)
        y_copies.append(
            send(partial.at[:, peer], part_y.at[step], ry_send.at[step], ry_recv.at[step], "gy", peer)
        )
        y_copies[-1].start()
    total = partial[:, gy]
    for i, copy in enumerate(y_copies):
        copy.wait_recv()
        total = total + part_y[i + 1]
    part_y[0] = total
    x_copies = []
    for step in range(1, n_gx):
        peer = lax.rem(gx + step, n_gx)
        x_copies.append(
            send(part_y.at[0, peer], part_x.at[step], rx_send.at[step], rx_recv.at[step], "gx", peer)
        )
        x_copies[-1].start()
    total = part_y[0, gx]
    for i, copy in enumerate(x_copies):
        copy.wait_recv()
        total = total + part_x[i + 1]
    out_rows = lax.broadcasted_iota(jnp.int32, (obs, padded), 0)
    out_lanes = lax.broadcasted_iota(jnp.int32, (obs, padded), 1)
    unpad = jnp.where((out_rows // owned) * PAD + lax.rem(out_rows, owned) == out_lanes, 1.0, 0.0)
    result = lax.dot_general(unpad, total, NT, precision=HIGHEST, preferred_element_type=F32)
    total_cells = rows_x * n_gx * size_y * layers
    jjt[...] = result[:, :owned] * (1.0 / float(total_cells))

    for copies in (cond_copies, head_copies, res_copies, app_copies):
        sent(copies)
    for copies in (a_gx, b_gx, a_gy, b_gy, y_copies, x_copies, [c for _, c in sens_copies]):
        for copy in copies:
            copy.wait_send()


def body(prior_heads, facies, facies_cond, well_cell, pump_rate, obs_test, obs_pair):
    n_gx, n_gy, n_ta = lax.axis_size("gx"), lax.axis_size("gy"), lax.axis_size("ta")
    group, rows_x, rows_y, layers = prior_heads.shape
    obs = obs_test.shape[0]
    cells = rows_x * rows_y
    owned = n_ta * obs // (n_gx * n_gy)
    padded = obs // owned * PAD
    own = (rows_x, rows_y, group, layers)
    at_x, at_y = (2, rows_y, group, layers), (2, rows_x, group, layers)
    f, b = (lambda shape: pltpu.VMEM(shape, F32)), (lambda shape: pltpu.VMEM(shape, BF16))
    wide = (group, 4 * group)
    sems = pltpu.SemaphoreType.DMA
    scratch = [
        f((cells, layers)), f((2, rows_y, layers)), f((2, 8, layers)), f((2, 8, layers)),
        f((15, cells, layers)),
        f(own), f(at_x), f(at_y),
        f(own), f(at_x), f(at_y),
        f(own), b(own), b(at_x), b(at_y), b(own),
        f(own),
        b(own), b(own), b(at_x), b(at_x), b(at_y), b(at_y),
        f(own), f(at_x), f(at_y),
        b((2 * padded, 128)), b((n_ta, CHUNKS, padded, cells // CHUNKS * layers)),
        f((n_gx, n_gy, PAD, padded)), f((n_gy, n_gx, PAD, padded)), f((n_gx, PAD, padded)),
        f((n_gx,) + wide), f((n_gy,) + wide), f((n_gx,) + wide), f((n_gy,) + wide),
        sems((4, 4)), sems((4, 4)),
        sems((2, n_gx)), sems((2, n_gx)), sems((2, n_gy)), sems((2, n_gy)),
        sems((n_gx,)), sems((n_gx,)), sems((n_gy,)), sems((n_gy,)),
        sems((n_ta, CHUNKS)), sems((n_ta, CHUNKS)),
    ]
    vmem, smem = pl.BlockSpec(memory_space=pltpu.VMEM), pl.BlockSpec(memory_space=pltpu.SMEM)
    heads, jjt = pl.pallas_call(
        functools.partial(kernel, (n_gx, n_gy, n_ta, group, rows_x, rows_y, layers, obs)),
        out_shape=(
            jax.ShapeDtypeStruct((group * cells, layers), F32),
            jax.ShapeDtypeStruct((obs, owned), F32),
        ),
        in_specs=[vmem, vmem, smem, smem, smem, smem, smem],
        out_specs=(vmem, vmem),
        scratch_shapes=scratch,
        compiler_params=pltpu.CompilerParams(
            collective_id=0, has_side_effects=True, vmem_limit_bytes=32 * 1024 * 1024
        ),
    )(
        prior_heads.reshape(group * cells, layers), facies.reshape(cells, layers),
        facies_cond, well_cell, pump_rate, obs_test, obs_pair,
    )
    return heads.reshape(prior_heads.shape), jjt


def solution(mesh):
    in_specs = (
        P("ta", "gx", "gy", None),
        P("gx", "gy", None),
        P(),
        P("ta"),
        P("ta"),
        P("ta"),
        P("ta"),
    )
    out_specs = (P("ta", "gx", "gy", None), P("ta", ("gx", "gy")))
    return jax.shard_map(body, mesh=mesh, in_specs=in_specs, out_specs=out_specs, check_vma=False)
```

time: 403 us -> 44.4 us (0.11)
  blocking collectives: 270 us -> 0 us
  starting transfers between devices: 66.3 us -> 0 us
  Pallas kernels: 0 us -> 39.8 us
  other arithmetic: 27.4 us -> 0 us
  waiting for transfers between devices: 15.5 us -> 0 us
  local copies, waits for them, and re-layouts: 15.5 us -> 3.7 us
  matrix products: 4.96 us -> 0 us
    psum x3 -> x0, blocking collectives: 227 us -> none  [reduced(): return lax.psum(gram_local(first_field, second_field), ('gx', 'gy'))]
    ppermute x20 -> x0, starting transfers between devices: 59.6 us -> none  [the longest x10 46.6 us: padded_2(): before = lax.ppermute(last, axis, up)]
    unnamed x1 -> x0, blocking collectives: 40.2 us -> none
    pallas_call x0 -> x1, Pallas kernels: none -> 39.8 us  [body(): pl.pallas_call(functools.partial(kernel, (n_gx, n_gy, n_ta, group, rows_x...]
    another operation x15 -> x0, other arithmetic: 20 us -> none  [the longest x9 10.8 us: solve_spd(): factor = jnp.linalg.cholesky(matrix)]
    ppermute x20 -> x0, waiting for transfers between devices: 15.5 us -> none  [the longest x10 8.87 us: padded_2(): before = lax.ppermute(last, axis, up)]
    gather x6 -> x0, local copies, waits for them, and re-layouts: 6.84 us -> none  [the longest x3 3.84 us: body(): jnp.take(gradient, second_local, axis=0)]
    unnamed x4 -> x0, starting transfers between devices: 6.73 us -> none
  transfers between devices with their start and end apart: 24 -> 0, of which waited for: 12 -> 0; matrix products, arithmetic and copies ran while one was open for 2% -> 0% of each run, Pallas kernels for 0% -> 0%
where the time goes in v1:
time: 44.4 us; the launch traced here: 44.2 us
  Pallas kernels  39.8 us (90%)
  local copies, waits for them, and re-layouts  3.7 us (8%)
  between operations  0.68 us (2%)
    pallas_call x1, Pallas kernels, body(): pl.pallas_call(functools.partial(kernel, (n_gx, n_gy, n_ta, group, rows_x...  39.8 us
    unnamed x16, local copies, waits for them, and re-layouts  3.7 us

profile of v1, /device:TPU:0, one launch (start us, length us, event | category | flops | bytes accessed | tf_op | source)
XLA Modules:
  0.0 44.2 jit_solution(2635421187236356687)
XLA Ops:
  0.6 0.0 copy-start.5
  0.6 0.0 copy-start.6
  0.7 0.0 copy-start.2
  0.7 0.0 copy-start.3
  0.7 0.0 copy-start.4
  0.7 0.6 %copy-done.5 = s32[96]{0:T(128)S(1)} copy-done((s32[96]{0:T(128)S(1)}, s32[96]{0:T(128)}, u32[]{:S(2)}) %copy-start.5) | copy-done | bytes 408
  1.3 0.0 copy-done.6
  1.3 0.0 copy-done.2
  1.3 0.0 copy-done.3
  1.3 0.0 copy-done.4
  1.4 0.0 copy-start
  1.4 0.9 %copy-done = f32[32,2,8,128]{3,2,1,0:T(8,128)S(1)} copy-done((f32[32,2,8,128]{3,2,1,0:T(8,128)S(1)}, f32[32,2,8,128]{3,2,1,0:T(8,128)}, u32[]{:S(2)}) %copy-start) | copy-done | bytes 262168
  2.3 0.0 copy-start.1
  2.3 0.7 %copy-done.1 = s32[2,8,128]{2,1,0:T(8,128)S(1)} copy-done((s32[2,8,128]{2,1,0:T(8,128)S(1)}, s32[2,8,128]{2,1,0:T(8,128)}, u32[]{:S(2)}) %copy-start.1) | copy-done | bytes 8216
  3.0 39.8 %shard_map.86 = (f32[512,128]{1,0:T(8,128)S(1)}, f32[96,12]{1,0:T(8,128)S(1)}) custom-call(f32[512,128]{1,0:T(8,128)S(1)} %bitcast.3, s32[16,128]{1,0:T(8,128)S(1)} %bitcast.5, f32[6]{0:T(128)S(1)} %copy-done.2, s32[32]{0:T(128)S(1)} %copy-done.3, f32[32]{0:T(128)S(1)} %copy-done.4, s32[96]{0:T(128)S(1)} %copy-done.5, s32[96]{0:T(128)S(1)} %copy-done.6), custom_call_target="tpu_custom_call" | custom-call | tf_op jit(solution)/shard_map/pallas_call | solution.py:455
  42.8 0.7 %copy.9 = f32[96,12]{0,1:T(8,128)} copy(f32[96,12]{1,0:T(8,128)S(1)} %get-tuple-element.7) | data formatting | bytes 9216
  43.5 0.7 %copy.11 = f32[32,2,8,128]{3,2,1,0:T(8,128)} copy(f32[32,2,8,128]{3,2,1,0:T(8,128)S(1)} %bitcast.4) | data formatting | bytes 524288
Async XLA Ops:
  0.6 0.7 %copy-start.5 = (s32[96]{0:T(128)S(1)}, s32[96]{0:T(128)}, u32[]{:S(2)}) copy-start(s32[96]{0:T(128)} %obs_test.1) | copy-start | bytes 1156
  0.6 0.7 %copy-start.6 = (s32[96]{0:T(128)S(1)}, s32[96]{0:T(128)}, u32[]{:S(2)}) copy-start(s32[96]{0:T(128)} %obs_pair.1) | copy-start | bytes 1156
  0.7 0.7 %copy-start.2 = (f32[6]{0:T(128)S(1)}, f32[6]{0:T(128)}, u32[]{:S(2)}) copy-start(f32[6]{0:T(128)} %facies_cond.1) | copy-start | bytes 76
  0.7 0.7 %copy-start.3 = (s32[32]{0:T(128)S(1)}, s32[32]{0:T(128)}, u32[]{:S(2)}) copy-start(s32[32]{0:T(128)} %well.1) | copy-start | bytes 388
  0.7 0.7 %copy-start.4 = (f32[32]{0:T(128)S(1)}, f32[32]{0:T(128)}, u32[]{:S(2)}) copy-start(f32[32]{0:T(128)} %rate.1) | copy-start | bytes 388
  1.4 0.9 %copy-start = (f32[32,2,8,128]{3,2,1,0:T(8,128)S(1)}, f32[32,2,8,128]{3,2,1,0:T(8,128)}, u32[]{:S(2)}) copy-start(f32[32,2,8,128]{3,2,1,0:T(8,128)} %param.7) | copy-start | bytes 786436
  2.3 0.7 %copy-start.1 = (s32[2,8,128]{2,1,0:T(8,128)S(1)}, s32[2,8,128]{2,1,0:T(8,128)}, u32[]{:S(2)}) copy-start(s32[2,8,128]{2,1,0:T(8,128)} %param.8) | copy-start | bytes 24580

commit v2 on v1

--- a/solution.py
+++ b/solution.py
@@ -45,11 +45,11 @@
     twice_f,
     res_h, res_l, res_xh, res_xl, res_yh, res_yl,
     fin_f, fin_x, fin_y,
-    pick, sens, partial, part_y, part_x,
-    sum_ax, sum_ay, sum_bx, sum_by,
+    pick, sens, partial, parts,
+    sum_ax, sum_ay, sum_b,
     halo_send, halo_recv,
     ax_send, ax_recv, ay_send, ay_recv,
-    rx_send, rx_recv, ry_send, ry_recv,
+    b_send, b_recv, p_send, p_recv,
     ta_send, ta_recv,
 ):
     n_gx, n_gy, n_ta, group, rows_x, rows_y, layers, obs = dims
@@ -62,17 +62,20 @@
     padded = owners * PAD
 
     barrier = pltpu.get_barrier_semaphore()
-    for axis, own, count in (("gx", gx, n_gx), ("gy", gy, n_gy), ("ta", ta, n_ta)):
-        for step in range(1, count):
-            pl.semaphore_signal(
-                barrier, inc=1, device_id={axis: lax.rem(own + step, count)},
-                device_id_type=pl.DeviceIdType.MESH,
-            )
+    tiles = n_gx * n_gy
+    own_tile = gx * n_gy + gy
+    steps = [(a, b) for a in range(n_gx) for b in range(n_gy) if a or b]
+    others = [{"gx": lax.rem(gx + a, n_gx), "gy": lax.rem(gy + b, n_gy)} for a, b in steps]
+    for peer in others + [{"ta": lax.rem(ta + step, n_ta)} for step in range(1, n_ta)]:
+        pl.semaphore_signal(barrier, inc=1, device_id=peer, device_id_type=pl.DeviceIdType.MESH)
 
     def send(src, dst, send_sem, recv_sem, axis, peer):
+        return send_to(src, dst, send_sem, recv_sem, {axis: peer})
+
+    def send_to(src, dst, send_sem, recv_sem, device):
         return pltpu.make_async_remote_copy(
             src_ref=src, dst_ref=dst, send_sem=send_sem, recv_sem=recv_sem,
-            device_id={axis: peer}, device_id_type=pl.DeviceIdType.MESH,
+            device_id=device, device_id_type=pl.DeviceIdType.MESH,
         )
 
     up_x, down_x = lax.rem(gx + 1, n_gx), lax.rem(gx + n_gx - 1, n_gx)
@@ -124,7 +127,7 @@
             for halo in ((cond_x, head_x, res_x, app_x) if side < 2 else (cond_y, head_y, res_y, app_y)):
                 halo[side % 2] = jnp.zeros(halo.shape[1:], halo.dtype)
 
-    pl.semaphore_wait(barrier, n_gx + n_gy + n_ta - 3)
+    pl.semaphore_wait(barrier, tiles + n_ta - 2)
     first_rows, last_rows = pl.ds(0, rows_y), pl.ds((rows_x - 1) * rows_y, rows_y)
     cond_copies = exchange(
         3, (cond.at[last_rows], cond.at[first_rows], cond_ys.at[0], cond_ys.at[1]), cond_x, cond_y
@@ -261,7 +264,7 @@
 
     a_gx = reduce_start(
         sum_ax, jnp.where(table_lane < 2 * group, gram[:group], gram[group:]),
-        "gx", gx, n_gx, ax_send.at[0], ax_recv.at[0],
+        "gx", gx, n_gx, ax_send, ax_recv,
     )
     for side in range(2):
         for y in range(rows_y):
@@ -283,11 +286,18 @@
     gram = lax.dot_general(left, jnp.concatenate(right, axis=1), NT, preferred_element_type=F32)
     gram = gram[:group] + gram[group:]
     gram = gram + pltpu.roll(gram, 2 * group, 1)
-    b_gx = reduce_start(sum_bx, gram, "gx", gx, n_gx, ax_send.at[1], ax_recv.at[1])
+    part = group // 4
+    part_lane = lax.broadcasted_iota(jnp.int32, (part, 4 * group), 1)
+    packed = gram[:part]
+    for i in range(1, 4):
+        packed = jnp.where(part_lane >= i * group, gram[i * part:(i + 1) * part], packed)
+    sum_b[own_tile] = packed
+    b_all = []
+    for i, peer in enumerate(others):
+        b_all.append(send_to(sum_b.at[own_tile], sum_b.at[own_tile], b_send.at[i], b_recv.at[i], peer))
+        b_all[-1].start()
     total = reduce_end(sum_ax, a_gx, n_gx)
-    a_gy = reduce_start(sum_ay, total, "gy", gy, n_gy, ay_send.at[0], ay_recv.at[0])
-    total = reduce_end(sum_bx, b_gx, n_gx)
-    b_gy = reduce_start(sum_by, total, "gy", gy, n_gy, ay_send.at[1], ay_recv.at[1])
+    a_gy = reduce_start(sum_ay, total, "gy", gy, n_gy, ay_send, ay_recv)
     first = reduce_end(sum_ay, a_gy, n_gy)
 
     before = first + (shift * SCALE) * pltpu.roll(first, group, 1)
@@ -300,7 +310,10 @@
         precision=HIGHEST, preferred_element_type=F32,
     )
     side = pltpu.roll(first, 3 * group, 1)
-    second = reduce_end(sum_by, b_gy, n_gy)
+    packed = reduce_end(sum_b, b_all, tiles)
+    second = jnp.concatenate(
+        [pltpu.roll(packed, (3 - i) * group, 1) if i < 3 else packed for i in range(4)], axis=0
+    )
     lower = eliminate(jnp.where(table_lane < group, side, second) - product, 3 * group, group)
     upper = after - lax.dot_general(
         jnp.where(keep, after, 0.0), jnp.concatenate([gap, lower], axis=0), NN,
@@ -375,49 +388,42 @@
     def gathered(index):
         return jnp.concatenate([sens[index, chunk] for chunk in range(CHUNKS)], axis=1)
 
+    mine = gathered(ta)
     for step in range(n_ta):
         for owner_step, copy in sens_copies:
             if owner_step == step:
                 copy.wait_recv()
         index = lax.rem(ta + n_ta - step, n_ta)
-        value = lax.dot_general(gathered(index), gathered(ta), NT, preferred_element_type=F32)
+        value = lax.dot_general(
+            mine if step == 0 else gathered(index), mine, NT, preferred_element_type=F32
+        )
         for k in range(owners):
             b = index * owners + k
-            partial[b // n_gy, lax.rem(b, n_gy)] = value[k * PAD:(k + 1) * PAD]
-
-    y_copies = []
-    for step in range(1, n_gy):
-        peer = lax.rem(gy + step, n_gy)
-        y_copies.append(
-            send(partial.at[:, peer], part_y.at[step], ry_send.at[step], ry_recv.at[step], "gy", peer)
-        )
-        y_copies[-1].start()
-    total = partial[:, gy]
-    for i, copy in enumerate(y_copies):
+            partial[b] = value[k * PAD:k * PAD + owned]
+            copy = send_to(
+                partial.at[b], parts.at[own_tile], p_send.at[b], p_recv.at[own_tile],
+                {"gx": b // n_gy, "gy": lax.rem(b, n_gy)},
+            )
+            pl.when(b != own_tile)(copy.start)
+    total = partial[own_tile]
+    part_copies = []
+    for i, (a, b) in enumerate(steps):
+        source = lax.rem(gx + n_gx - a, n_gx) * n_gy + lax.rem(gy + n_gy - b, n_gy)
+        target = others[i]["gx"] * n_gy + others[i]["gy"]
+        copy = send_to(partial.at[target], parts.at[source], p_send.at[target], p_recv.at[source], others[i])
         copy.wait_recv()
-        total = total + part_y[i + 1]
-    part_y[0] = total
-    x_copies = []
-    for step in range(1, n_gx):
-        peer = lax.rem(gx + step, n_gx)
-        x_copies.append(
-            send(part_y.at[0, peer], part_x.at[step], rx_send.at[step], rx_recv.at[step], "gx", peer)
-        )
-        x_copies[-1].start()
-    total = part_y[0, gx]
-    for i, copy in enumerate(x_copies):
-        copy.wait_recv()
-        total = total + part_x[i + 1]
+        part_copies.append(copy)
+        total = total + parts[source]
     out_rows = lax.broadcasted_iota(jnp.int32, (obs, padded), 0)
     out_lanes = lax.broadcasted_iota(jnp.int32, (obs, padded), 1)
     unpad = jnp.where((out_rows // owned) * PAD + lax.rem(out_rows, owned) == out_lanes, 1.0, 0.0)
-    result = lax.dot_general(unpad, total, NT, precision=HIGHEST, preferred_element_type=F32)
+    result = lax.dot_general(total, unpad, NT, precision=HIGHEST, preferred_element_type=F32)
     total_cells = rows_x * n_gx * size_y * layers
-    jjt[...] = result[:, :owned] * (1.0 / float(total_cells))
+    jjt[...] = result * (1.0 / float(total_cells))
 
     for copies in (cond_copies, head_copies, res_copies, app_copies):
         sent(copies)
-    for copies in (a_gx, b_gx, a_gy, b_gy, y_copies, x_copies, [c for _, c in sens_copies]):
+    for copies in (a_gx, a_gy, b_all, part_copies, [c for _, c in sens_copies]):
         for copy in copies:
             copy.wait_send()
 
@@ -433,6 +439,7 @@
     at_x, at_y = (2, rows_y, group, layers), (2, rows_x, group, layers)
     f, b = (lambda shape: pltpu.VMEM(shape, F32)), (lambda shape: pltpu.VMEM(shape, BF16))
     wide = (group, 4 * group)
+    tiles = n_gx * n_gy
     sems = pltpu.SemaphoreType.DMA
     scratch = [
         f((cells, layers)), f((2, rows_y, layers)), f((2, 8, layers)), f((2, 8, layers)),
@@ -444,11 +451,11 @@
         b(own), b(own), b(at_x), b(at_x), b(at_y), b(at_y),
         f(own), f(at_x), f(at_y),
         b((2 * padded, 128)), b((n_ta, CHUNKS, padded, cells // CHUNKS * layers)),
-        f((n_gx, n_gy, PAD, padded)), f((n_gy, n_gx, PAD, padded)), f((n_gx, PAD, padded)),
-        f((n_gx,) + wide), f((n_gy,) + wide), f((n_gx,) + wide), f((n_gy,) + wide),
+        f((tiles, owned, padded)), f((tiles, owned, padded)),
+        f((n_gx,) + wide), f((n_gy,) + wide), f((tiles, group // 4, 4 * group)),
         sems((4, 4)), sems((4, 4)),
-        sems((2, n_gx)), sems((2, n_gx)), sems((2, n_gy)), sems((2, n_gy)),
         sems((n_gx,)), sems((n_gx,)), sems((n_gy,)), sems((n_gy,)),
+        sems((tiles,)), sems((tiles,)), sems((tiles,)), sems((tiles,)),
         sems((n_ta, CHUNKS)), sems((n_ta, CHUNKS)),
     ]
     vmem, smem = pl.BlockSpec(memory_space=pltpu.VMEM), pl.BlockSpec(memory_space=pltpu.SMEM)
@@ -456,7 +463,7 @@
         functools.partial(kernel, (n_gx, n_gy, n_ta, group, rows_x, rows_y, layers, obs)),
         out_shape=(
             jax.ShapeDtypeStruct((group * cells, layers), F32),
-            jax.ShapeDtypeStruct((obs, owned), F32),
+            jax.ShapeDtypeStruct((owned, obs), F32),
         ),
         in_specs=[vmem, vmem, smem, smem, smem, smem, smem],
         out_specs=(vmem, vmem),
@@ -468,7 +475,7 @@
         prior_heads.reshape(group * cells, layers), facies.reshape(cells, layers),
         facies_cond, well_cell, pump_rate, obs_test, obs_pair,
     )
-    return heads.reshape(prior_heads.shape), jjt
+    return heads.reshape(prior_heads.shape), jjt.T
 
 
 def solution(mesh):

time: 44.4 us -> 43 us (0.968)
  Pallas kernels: 39.8 us -> 38.4 us
    pallas_call x1, Pallas kernels: 39.8 us -> 38.4 us  [body(): pl.pallas_call(functools.partial(kernel, (n_gx, n_gy, n_ta, group, rows_x...]
where the time goes in v2:
time: 43 us; the launch traced here: 42.7 us
  Pallas kernels  38.4 us (89%)
  local copies, waits for them, and re-layouts  3.63 us (8%)
  between operations  0.68 us (2%)
    pallas_call x1, Pallas kernels, body(): pl.pallas_call(functools.partial(kernel, (n_gx, n_gy, n_ta, group, rows_x...  38.4 us
    unnamed x16, local copies, waits for them, and re-layouts  3.63 us

profile of v2, /device:TPU:0, one launch (start us, length us, event | category | flops | bytes accessed | tf_op | source)
XLA Modules:
  0.0 42.7 jit_solution(18301276530291694387)
XLA Ops:
  0.6 0.0 copy-start.5
  0.6 0.0 copy-start.6
  0.7 0.0 copy-start.2
  0.7 0.0 copy-start.3
  0.7 0.0 copy-start.4
  0.7 0.6 %copy-done.5 = s32[96]{0:T(128)S(1)} copy-done((s32[96]{0:T(128)S(1)}, s32[96]{0:T(128)}, u32[]{:S(2)}) %copy-start.5) | copy-done | bytes 408
  1.3 0.0 copy-done.6
  1.3 0.0 copy-done.2
  1.3 0.0 copy-done.3
  1.3 0.0 copy-done.4
  1.4 0.0 copy-start
  1.4 0.9 %copy-done = f32[32,2,8,128]{3,2,1,0:T(8,128)S(1)} copy-done((f32[32,2,8,128]{3,2,1,0:T(8,128)S(1)}, f32[32,2,8,128]{3,2,1,0:T(8,128)}, u32[]{:S(2)}) %copy-start) | copy-done | bytes 262168
  2.3 0.0 copy-start.1
  2.3 0.7 %copy-done.1 = s32[2,8,128]{2,1,0:T(8,128)S(1)} copy-done((s32[2,8,128]{2,1,0:T(8,128)S(1)}, s32[2,8,128]{2,1,0:T(8,128)}, u32[]{:S(2)}) %copy-start.1) | copy-done | bytes 8216
  3.0 38.4 %shard_map.86 = (f32[512,128]{1,0:T(8,128)S(1)}, f32[12,96]{1,0:T(8,128)S(1)}) custom-call(f32[512,128]{1,0:T(8,128)S(1)} %bitcast.4, s32[16,128]{1,0:T(8,128)S(1)} %bitcast.6, f32[6]{0:T(128)S(1)} %copy-done.2, s32[32]{0:T(128)S(1)} %copy-done.3, f32[32]{0:T(128)S(1)} %copy-done.4, s32[96]{0:T(128)S(1)} %copy-done.5, s32[96]{0:T(128)S(1)} %copy-done.6), custom_call_target="tpu_custom_call" | custom-call | tf_op jit(solution)/shard_map/pallas_call | solution.py:462
  41.4 0.7 %copy.11 = f32[32,2,8,128]{3,2,1,0:T(8,128)} copy(f32[32,2,8,128]{3,2,1,0:T(8,128)S(1)} %bitcast.5) | data formatting | bytes 524288
  42.1 0.6 %copy.12 = f32[96,12]{0,1:T(8,128)} copy(f32[96,12]{0,1:T(8,128)S(1)} %bitcast.7) | data formatting | bytes 9216
Async XLA Ops:
  0.6 0.7 %copy-start.5 = (s32[96]{0:T(128)S(1)}, s32[96]{0:T(128)}, u32[]{:S(2)}) copy-start(s32[96]{0:T(128)} %obs_test.1) | copy-start | bytes 1156
  0.6 0.7 %copy-start.6 = (s32[96]{0:T(128)S(1)}, s32[96]{0:T(128)}, u32[]{:S(2)}) copy-start(s32[96]{0:T(128)} %obs_pair.1) | copy-start | bytes 1156
  0.7 0.7 %copy-start.2 = (f32[6]{0:T(128)S(1)}, f32[6]{0:T(128)}, u32[]{:S(2)}) copy-start(f32[6]{0:T(128)} %facies_cond.1) | copy-start | bytes 76
  0.7 0.7 %copy-start.3 = (s32[32]{0:T(128)S(1)}, s32[32]{0:T(128)}, u32[]{:S(2)}) copy-start(s32[32]{0:T(128)} %well.1) | copy-start | bytes 388
  0.7 0.7 %copy-start.4 = (f32[32]{0:T(128)S(1)}, f32[32]{0:T(128)}, u32[]{:S(2)}) copy-start(f32[32]{0:T(128)} %rate.1) | copy-start | bytes 388
  1.4 0.9 %copy-start = (f32[32,2,8,128]{3,2,1,0:T(8,128)S(1)}, f32[32,2,8,128]{3,2,1,0:T(8,128)}, u32[]{:S(2)}) copy-start(f32[32,2,8,128]{3,2,1,0:T(8,128)} %param.7) | copy-start | bytes 786436
  2.3 0.7 %copy-start.1 = (s32[2,8,128]{2,1,0:T(8,128)S(1)}, s32[2,8,128]{2,1,0:T(8,128)}, u32[]{:S(2)}) copy-start(s32[2,8,128]{2,1,0:T(8,128)} %param.8) | copy-start | bytes 24580

commit v3 on v2

--- a/solution.py
+++ b/solution.py
@@ -13,6 +13,7 @@
 BF16 = jnp.bfloat16
 HIGHEST = lax.Precision.HIGHEST
 CHUNKS = 4
+BLOCK = 4
 PAD = 16
 NT = (((1,), (1,)), ((), ()))
 NN = (((1,), (0,)), ((), ()))
@@ -24,19 +25,34 @@
 
 
 def eliminate(table, first_lane, size):
-    rows = lax.broadcasted_iota(jnp.int32, table.shape, 0)
-    for k in range(size):
-        lane = first_lane + k
-        column = table[:, lane:lane + 1]
-        pivot = table[k:k + 1, lane:lane + 1]
-        scaled = table[k:k + 1, :] * (1.0 / pivot)
-        table = jnp.where(rows == k, scaled, table - column * scaled)
+    index = lax.broadcasted_iota(jnp.int32, table.shape, 0)
+    for k in range(0, size, BLOCK):
+        columns = [
+            jnp.broadcast_to(table[:, first_lane + k + j:first_lane + k + j + 1], table.shape)
+            for j in range(BLOCK)
+        ]
+        rows = [table[k + i:k + i + 1, :] for i in range(BLOCK)]
+        corner = [[columns[j][k + i:k + i + 1, :] for j in range(BLOCK)] for i in range(BLOCK)]
+        for i in range(BLOCK):
+            inverse = 1.0 / corner[i][i]
+            rows[i] = rows[i] * inverse
+            for j in range(i + 1, BLOCK):
+                corner[i][j] = corner[i][j] * inverse
+            for m in range(BLOCK):
+                if m != i:
+                    rows[m] = rows[m] - corner[m][i] * rows[i]
+                    for j in range(i + 1, BLOCK):
+                        corner[m][j] = corner[m][j] - corner[m][i] * corner[i][j]
+        for j in range(BLOCK):
+            table = table - columns[j] * rows[j]
+        for j in range(BLOCK):
+            table = jnp.where(index == k + j, rows[j], table)
     return table
 
 
 def kernel(
     dims,
-    prior, facies, facies_cond, well, rate, obs_test, obs_pair,
+    prior_in, facies_in, facies_cond, well, rate, obs_test, obs_pair,
     heads, jjt,
     cond, cond_x, cond_y, cond_ys, weights,
     head_f, head_x, head_y,
@@ -47,6 +63,7 @@
     fin_f, fin_x, fin_y,
     pick, sens, partial, parts,
     sum_ax, sum_ay, sum_b,
+    prior, facies, in_sem,
     halo_send, halo_recv,
     ax_send, ax_recv, ay_send, ay_recv,
     b_send, b_recv, p_send, p_recv,
@@ -61,6 +78,12 @@
     owners = obs // owned
     padded = owners * PAD
 
+    loads = [
+        pltpu.make_async_copy(facies_in, facies, in_sem.at[0]),
+        pltpu.make_async_copy(prior_in, prior, in_sem.at[1]),
+    ]
+    for load in loads:
+        load.start()
     barrier = pltpu.get_barrier_semaphore()
     tiles = n_gx * n_gy
     own_tile = gx * n_gy + gy
@@ -107,6 +130,7 @@
     def faces(field):
         return (field.at[rows_x - 1], field.at[0], field.at[:, rows_y - 1], field.at[:, 0])
 
+    loads[0].wait()
     kinds = facies[...]
     conduct = jnp.zeros(kinds.shape, F32)
     mean = jnp.float32(0.0)
@@ -119,6 +143,7 @@
         cond_ys[0, x:x + 1, :] = conduct[(x + 1) * rows_y - 1:(x + 1) * rows_y]
         cond_ys[1, x:x + 1, :] = conduct[x * rows_y:x * rows_y + 1]
     shift = STORAGE + mean * (9.0 / facies_cond.shape[0])
+    loads[1].wait()
     for x, y in blocks:
         head_f[x, y] = prior[pl.ds(x * rows_y + y, group, stride=cells), :]
     for side, low in enumerate(lows):
@@ -276,6 +301,8 @@
     left = jnp.concatenate(
         [jnp.concatenate([app_b[x, y], app_l[x, y]], axis=0) for x, y in blocks], axis=1
     )
+    total = reduce_end(sum_ax, a_gx, n_gx)
+    a_gy = reduce_start(sum_ay, total, "gy", gy, n_gy, ay_send, ay_recv)
     arrived(app_copies)
     right = []
     for x, y in blocks:
@@ -296,8 +323,6 @@
     for i, peer in enumerate(others):
         b_all.append(send_to(sum_b.at[own_tile], sum_b.at[own_tile], b_send.at[i], b_recv.at[i], peer))
         b_all[-1].start()
-    total = reduce_end(sum_ax, a_gx, n_gx)
-    a_gy = reduce_start(sum_ay, total, "gy", gy, n_gy, ay_send, ay_recv)
     first = reduce_end(sum_ay, a_gy, n_gy)
 
     before = first + (shift * SCALE) * pltpu.roll(first, group, 1)
@@ -453,23 +478,25 @@
         b((2 * padded, 128)), b((n_ta, CHUNKS, padded, cells // CHUNKS * layers)),
         f((tiles, owned, padded)), f((tiles, owned, padded)),
         f((n_gx,) + wide), f((n_gy,) + wide), f((tiles, group // 4, 4 * group)),
+        f((group * cells, layers)), pltpu.VMEM((cells, layers), jnp.int32), sems((2,)),
         sems((4, 4)), sems((4, 4)),
         sems((n_gx,)), sems((n_gx,)), sems((n_gy,)), sems((n_gy,)),
         sems((tiles,)), sems((tiles,)), sems((tiles,)), sems((tiles,)),
         sems((n_ta, CHUNKS)), sems((n_ta, CHUNKS)),
     ]
     vmem, smem = pl.BlockSpec(memory_space=pltpu.VMEM), pl.BlockSpec(memory_space=pltpu.SMEM)
+    anywhere = pl.BlockSpec(memory_space=pl.ANY)
     heads, jjt = pl.pallas_call(
         functools.partial(kernel, (n_gx, n_gy, n_ta, group, rows_x, rows_y, layers, obs)),
         out_shape=(
             jax.ShapeDtypeStruct((group * cells, layers), F32),
             jax.ShapeDtypeStruct((owned, obs), F32),
         ),
-        in_specs=[vmem, vmem, smem, smem, smem, smem, smem],
+        in_specs=[anywhere, anywhere, smem, smem, smem, smem, smem],
         out_specs=(vmem, vmem),
         scratch_shapes=scratch,
         compiler_params=pltpu.CompilerParams(
-            collective_id=0, has_side_effects=True, vmem_limit_bytes=32 * 1024 * 1024
+            collective_id=0, has_side_effects=True, vmem_limit_bytes=56 * 1024 * 1024
         ),
     )(
         prior_heads.reshape(group * cells, layers), facies.reshape(cells, layers),

time: 43 us -> 39.5 us (0.919)
  Pallas kernels: 38.4 us -> 36.3 us
  local copies, waits for them, and re-layouts: 3.63 us -> 2.28 us
    pallas_call x1, Pallas kernels: 38.4 us -> 36.3 us  [body(): pl.pallas_call(functools.partial(kernel, (n_gx, n_gy, n_ta, group, rows_x...]
    unnamed x16 -> x4, local copies, waits for them, and re-layouts: 3.63 us -> 2.28 us
where the time goes in v3:
time: 39.5 us; the launch traced here: 39.2 us
  Pallas kernels  36.3 us (92%)
  local copies, waits for them, and re-layouts  2.28 us (6%)
  between operations  0.65 us (2%)
    pallas_call x1, Pallas kernels, body(): pl.pallas_call(functools.partial(kernel, (n_gx, n_gy, n_ta, group, rows_x...  36.3 us
    unnamed x4, local copies, waits for them, and re-layouts  2.28 us

profile of v3, /device:TPU:0, one launch (start us, length us, event | category | flops | bytes accessed | tf_op | source)
XLA Modules:
  0.0 39.2 jit_solution(11149594683756358867)
XLA Ops:
  0.6 36.3 %shard_map.86 = (f32[512,128]{1,0:T(8,128)}, f32[12,96]{1,0:T(8,128)}) custom-call(f32[512,128]{1,0:T(8,128)} %bitcast.4, s32[16,128]{1,0:T(8,128)} %bitcast.6, f32[6]{0:T(128)} %facies_cond.1, s32[32]{0:T(128)} %well.1, f32[32]{0:T(128)} %rate.1, s32[96]{0:T(128)} %obs_test.1, s32[96]{0:T(128)} %obs_pair.1), custom_call_target="tpu_custom_call" | custom-call | tf_op jit(solution)/shard_map/pallas_call | solution.py:489
  36.9 0.0 copy-start
  37.0 1.7 %copy.11 = f32[32,2,8,128]{3,2,1,0:T(8,128)} copy(f32[32,2,8,128]{3,2,1,0:T(8,128)} %bitcast.5) | data formatting | bytes 524288
  38.6 0.0 copy-done
  38.6 0.6 %copy.12 = f32[96,12]{0,1:T(8,128)} copy(f32[96,12]{0,1:T(8,128)S(1)} %bitcast.7) | data formatting | bytes 9216
Async XLA Ops:
  36.9 1.7 %copy-start = (f32[12,96]{1,0:T(8,128)S(1)}, f32[12,96]{1,0:T(8,128)}, u32[]{:S(2)}) copy-start(f32[12,96]{1,0:T(8,128)} %get-tuple-element.5) | copy-start | bytes 13828
